TPU v7x, 32 devices: a whole 2x2x4 slice. The times are simulated.
32 devices in a mesh: outer: 2 (over x), sec: 8 (over z, core), tp: 2 (over y).
Axes of the slice: x: 2, y: 2, z: 4, core: 2. Of those that a mesh axis runs over, the one named last changes fastest.
Arguments:
- tile_maps: bfloat16 [32, 12, 12, 3072], P(('outer', 'sec'), None, None, 'tp'), may hold values from -6 to 6
- tile_shape: int32 [32, 2], P(('outer', 'sec')), may hold values from 4 to 12
- conv_kernel: float32 [7, 7, 3072], P(None, None, 'tp'), may hold values from -0.875 to 0.875
- norm_gain: float32 [3072], P('tp'), may hold values from 0.25 to 1.75
- norm_bias: float32 [3072], P('tp'), may hold values from -3 to 3
- projector: bfloat16 [3072, 7168], P('tp', 'sec'), may hold values from -0.109375 to 0.109375
- text_rows: bfloat16 [9216, 7168], P(('outer', 'sec'), 'tp'), may hold values from -6 to 6
- row_order: int32 [16, 576], P(('outer', 'sec')), may hold values from 0 to 575, each once within a row
- seq_gain: float32 [7168], P('tp'), may hold values from 0.25 to 1.75
- cotangent: bfloat16 [9216, 7168], P(('outer', 'sec'), 'tp'), may hold values from -0.2772166 to 0.2772166, as said below
Outputs:
- normed: bfloat16 [9216, 7168], P(('outer', 'sec'), 'tp')
- kernel_delta: float32 [7, 7, 3072], P(None, None, 'tp')
- gain_delta: float32 [3072], P('tp')
- bias_delta: float32 [3072], P('tp')
Inputs may be any that keep to these rules, and one draw needn't show every extreme that they name: `row_order`: each row lists where the visual tokens arriving at that device stand, in arrival order, then the text rows. `tile_shape`: valid rows and columns of each tile, the rest of the map is padding. `cotangent`: gradient of the training loss.
All inputs are finite; a program needn't handle non-finite values.
Results may differ from a plain program's by a relative error of at most 0.0043.
Values may be sent and summed in bfloat16 or wider, within the bound.
A program may use at most 128 MiB of HBM per device.

v0:
```python
import jax
import jax.numpy as jnp
from jax import lax
from jax.sharding import PartitionSpec as P


def shape_mask(tile_shape, grid):
    places = lax.broadcasted_iota(jnp.int32, (1, grid), 1)
    rows_ok = places < tile_shape[:, 0:1]
    cols_ok = places < tile_shape[:, 1:2]
    return (rows_ok[:, :, None] & cols_ok[:, None, :]).astype(jnp.float32)


def on_device(
    tile_maps,
    tile_shape,
    conv_kernel,
    norm_gain,
    norm_bias,
    projector,
    text_rows,
    row_order,
    seq_gain,
    cotangent,
):
    grid = tile_maps.shape[1]
    half_ch = tile_maps.shape[3]
    channels = half_ch * lax.axis_size("tp")
    rows_dev = tile_maps.shape[0] * grid * grid
    width = text_rows.shape[1] * lax.axis_size("tp")
    validity = shape_mask(tile_shape, grid)[..., None]
    masked = tile_maps.astype(jnp.float32) * validity
    padded = jnp.pad(masked, ((0, 0), (3, 3), (3, 3), (0, 0)))
    conv_out = jnp.zeros(masked.shape, jnp.float32)
    for row_off in range(7):
        for col_off in range(7):
            conv_out = (
                conv_out
                + padded[:, row_off : row_off + grid, col_off : col_off + grid, :]
                * conv_kernel[row_off, col_off]
            )
    total_one, total_two = lax.psum(
        (jnp.sum(conv_out, axis=-1), jnp.sum(conv_out * conv_out, axis=-1)), "tp"
    )
    center = (total_one / channels)[..., None]
    inverse = lax.rsqrt((total_two / channels)[..., None] - center * center + 1e-06)
    normal = (conv_out - center) * inverse
    features = (
        (validity * (normal * norm_gain + norm_bias))
        .astype(jnp.bfloat16)
        .reshape(rows_dev, half_ch)
    )
    whole_weight = lax.all_gather(projector, "sec", axis=1, tiled=True)
    partial_value = jnp.dot(features, whole_weight, preferred_element_type=jnp.float32)
    visual = lax.psum_scatter(partial_value, "tp", scatter_dimension=1, tiled=True).astype(
        jnp.bfloat16
    )
    arrived = lax.all_to_all(visual, "sec", split_axis=0, concat_axis=0, tiled=True)
    positions = row_order[0, :rows_dev]
    merged = text_rows.at[positions].set(arrived)
    wide = merged.astype(jnp.float32)
    upstream = cotangent.astype(jnp.float32) * seq_gain
    square_sum, along = lax.psum(
        (jnp.sum(wide * wide, axis=-1), jnp.sum(upstream * wide, axis=-1)), "tp"
    )
    inv_rms = lax.rsqrt(square_sum / width + 1e-05)[:, None]
    normed = (wide * inv_rms * seq_gain).astype(jnp.bfloat16)
    grad_seq = inv_rms * upstream - wide * (inv_rms * inv_rms * inv_rms) * along[:, None] / width
    picked = grad_seq[positions].astype(jnp.bfloat16)
    returned = lax.all_to_all(picked, "sec", split_axis=0, concat_axis=0, tiled=True)
    full_grad = lax.all_gather(returned, "tp", axis=1, tiled=True)
    grad_rows = jnp.dot(full_grad, whole_weight.T, preferred_element_type=jnp.float32)
    masked_grad = grad_rows.reshape(masked.shape) * validity
    scaled = masked_grad * norm_gain
    first_sum, second_sum = lax.psum(
        (jnp.sum(scaled, axis=-1), jnp.sum(scaled * normal, axis=-1)), "tp"
    )
    grad_conv = inverse * (
        scaled - (first_sum / channels)[..., None] - normal * (second_sum / channels)[..., None]
    )
    kernel_rows = []
    for row_off in range(7):
        for col_off in range(7):
            window = padded[:, row_off : row_off + grid, col_off : col_off + grid, :]
            kernel_rows.append(jnp.sum(window * grad_conv, axis=(0, 1, 2)))
    gain_grad = jnp.sum(masked_grad * normal, axis=(0, 1, 2))
    bias_grad = jnp.sum(masked_grad, axis=(0, 1, 2))
    local_delta = jnp.stack(kernel_rows + [gain_grad, bias_grad], axis=0)
    pods = lax.axis_size("outer")
    entries = 51 * channels
    pod_sum = lax.psum(local_delta, "sec")
    norm_sq = lax.psum(jnp.sum(pod_sum * pod_sum), "tp")
    factor = jnp.minimum(1.0, 1.0 / jnp.sqrt(norm_sq / entries + 1e-06))
    average = lax.psum(pod_sum * factor, "outer") / pods
    return (normed, average[:49].reshape(7, 7, half_ch), average[49], average[50])


def solution(mesh):
    in_specs = (
        P(("outer", "sec"), None, None, "tp"),
        P(("outer", "sec"), None),
        P(None, None, "tp"),
        P("tp"),
        P("tp"),
        P("tp", "sec"),
        P(("outer", "sec"), "tp"),
        P(("outer", "sec"), None),
        P("tp"),
        P(("outer", "sec"), "tp"),
    )
    out_specs = (P(("outer", "sec"), "tp"), P(None, None, "tp"), P("tp"), P("tp"))
    return jax.shard_map(
        on_device, mesh=mesh, in_specs=in_specs, out_specs=out_specs, check_vma=False
    )
```

profile of v0, /device:TPU:0, one launch (start us, length us, event | category | flops | bytes accessed | tf_op | source)
XLA Modules:
  0.0 696.8 jit_solution(15552070662868830435)
XLA Ops:
  7.2 0.0 all-gather.3.cloned.1.call-start
  7.2 4.4 copy.23
  11.6 0.0 all-gather.3.cloned.1.call-update
  11.7 0.0 reduce-scatter.2.cloned.1.call-start
  11.7 0.6 copy-done.9
  12.3 0.2 slice_reduce_fusion.52
  12.5 0.1 copy-done.2
  12.6 0.2 slice_reduce_fusion.48
  12.8 0.3 slice_reduce_fusion.50
  13.1 0.9 slice_reduce_fusion.49
  14.0 0.1 iota_compare_fusion
  14.1 0.1 and_convert_fusion
  14.2 0.2 convert_multiply_fusion.5
  14.4 23.6 %fusion.8 = (f32[2,12,12]{2,1,0:T(8,128)S(1)}, f32[2,12,12]{2,1,0:T(8,128)S(1)}, f32[2,12,12,1536]{3,2,1,0:T(8,128)}) fusion(f32[1536]{0:T(1024)S(1)} %get-tuple-element.110, f32[1536]{0:T(1024)S(1)} %get-tuple-element.111, f32[1536]{0:T(1024)S(1)} %get-tuple-element.64, f32[1536]{0:T(1024)S(1)} %get-tuple-element.65, f32[1536]{0:T(1024)S(1)} %get-tuple-element.66, ...), kind=kLoop, calls=%fused_computation.189 | loop fusion | flops 44236224 | bytes 3842304 | tf_op jit(solution)/shard_map/reduce_sum | solution.py:43
  38.1 9.8 %all-reduce.3 = (f32[2,12,12]{2,1,0:T(8,128)S(1)}, f32[2,12,12]{2,1,0:T(8,128)S(1)}) all-reduce(f32[2,12,12]{2,1,0:T(8,128)S(1)} %get-tuple-element.58, f32[2,12,12]{2,1,0:T(8,128)S(1)} %get-tuple-element.57), channel_id=1, replica_groups=mesh['outer'=2,'sec'=8,'tp'=2] {'tp'}, use_global_device_ids=true, to_apply=%region_3.4 | all-reduce | flops 576 | bytes 4608 | tf_op jit(solution)/shard_map/psum | solution.py:42
  47.9 0.0 copy-start.5
  47.9 0.6 copy-done.3
  48.5 0.0 copy-done.5
  48.5 3.5 multiply_convert_fusion
  52.0 1.1 reshape.168
  53.1 155.4 %all-gather.3.cloned.1.call-done = bf16[1536,7168]{1,0:T(8,128)(2,1)} async-done(((bf16[1536,896]{1,0:T(8,128)(2,1)}), bf16[1536,7168]{1,0:T(8,128)(2,1)}) %all-gather.3.cloned.1.call-update) | async-done | bytes 22020112 | tf_op jit(solution)/shard_map/all_gather | solution.py:53
  208.5 13.1 %fusion.9 = f32[288,7168]{1,0:T(8,128)} fusion(bf16[288,1536]{1,0:T(8,128)(2,1)} %reshape.168, bf16[1536,7168]{1,0:T(8,128)(2,1)} %all-gather.3.cloned.1.call-done), kind=kOutput, calls=%fused_computation.190 | convolution fusion | flops 6341787648 | bytes 31162368 | tf_op jit(solution)/shard_map/dot_general | solution.py:54
  221.7 0.0 reduce-scatter.2.cloned.1.call-update
  221.7 96.2 %reduce-scatter.2.cloned.1.call-done = f32[288,3584]{1,0:T(8,128)} async-done(((f32[288,7168]{1,0:T(8,128)}), f32[288,3584]{1,0:T(8,128)}) %reduce-scatter.2.cloned.1.call-update) | async-done | bytes 4128784 | tf_op jit(solution)/shard_map/reduce_scatter | solution.py:55
  317.8 3.7 convert_element_type.43
  321.6 4.0 all_to_all.14
  325.5 4.7 all-to-all-start
  330.3 0.2 all-gather.5.cloned.1.call-start
  330.5 53.1 %all-to-all-done = bf16[8,36,3584]{2,1,0:T(8,128)(2,1)} async-done(((bf16[8,36,3584]{2,1,0:T(8,128)(2,1)}), bf16[8,36,3584]{2,1,0:T(8,128)(2,1)}, u32[]{:S(2)}, u32[]{:S(2)}) %all-to-all-start) | async-done | bytes 2064416 | tf_op jit(solution)/shard_map/all_to_all | solution.py:58
  383.7 4.0 reshape.184
  387.7 9.2 %scatter_fusion = bf16[576,3584]{1,0:T(8,128)(2,1)} fusion(bf16[576,3584]{1,0:T(8,128)(2,1)} %copy.23, s32[288]{0:T(512)S(1)} %fusion.7, bf16[288,3584]{1,0:T(8,128)(2,1)} %reshape.184), kind=kCustom, calls=%fused_computation.1 | custom fusion | bytes 6194304 | tf_op jit(solution)/shard_map/scatter | solution.py:60
  396.9 5.4 fusion.6
  402.3 5.0 all-reduce.2
  407.3 6.7 fusion.5
  414.0 10.0 %gather_fusion = bf16[288,3584]{1,0:T(8,128)(2,1)} fusion(bf16[576,3584]{1,0:T(8,128)(2,1)} %fusion.5, s32[1024]{0:T(1024)S(1)} %pad_clamp_fusion), kind=kCustom, calls=%fused_computation | custom fusion | bytes 4129920 | tf_op jit(solution)/shard_map/gather | solution.py:69
  424.1 4.0 convert_element_type.48
  428.0 57.6 %all_to_all.21 = bf16[8,36,3584]{2,1,0:T(8,128)(2,1)} all-to-all(bf16[8,36,3584]{2,1,0:T(8,128)(2,1)} %convert_element_type.48), channel_id=1, replica_groups=mesh['outer'=2,'sec'=8,'tp'=2] {'sec'}, dimensions={0} | all-to-all | bytes 4128768 | tf_op jit(solution)/shard_map/all_to_all | solution.py:70
  485.7 4.0 all_to_all.18
  489.6 0.0 all-gather.5.cloned.1.call-update
  489.6 0.0 all-reduce.7.cloned.1.call-start
  489.7 0.1 reshape.171
  489.8 54.0 %all-gather.5.cloned.1.call-done = bf16[288,7168]{1,0:T(8,128)(2,1)} async-done(((bf16[288,3584]{1,0:T(8,128)(2,1)}), bf16[288,7168]{1,0:T(8,128)(2,1)}) %all-gather.5.cloned.1.call-update) | async-done | bytes 4128784 | tf_op jit(solution)/shard_map/all_gather | solution.py:71
  543.7 13.2 %multiply_reduce_fusion.53 = (f32[1536]{0:T(1024)S(1)}, f32[288]{0:T(512)S(1)}, f32[288,1536]{1,0:T(8,128)}) fusion(f32[288]{0:T(512)S(1)} %reshape.171, f32[1536]{0:T(1024)S(1)} %copy-done.8, bf16[288,7168]{1,0:T(8,128)(2,1)} %all-gather.5.cloned.1.call-done, bf16[1536,7168]{1,0:T(8,128)(2,1)} %all-gather.3.cloned.1.call-done), kind=kOutput, calls=%fused_computation.120 | convolution fusion | flops 6343555072 | bytes 27932928 | tf_op jit(solution)/shard_map/dot_general | solution.py:72
  557.0 2.8 reshape.169
  559.8 3.4 multiply_reduce_fusion
  563.1 0.1 reduce_sum.529
  563.2 7.4 %all-reduce.1 = (f32[2,12,12]{2,1,0:T(8,128)S(1)}, f32[2,12,12]{2,1,0:T(8,128)S(1)}) all-reduce(f32[2,12,12]{2,1,0:T(8,128)S(1)} %get-tuple-element.5, f32[2,12,12]{2,1,0:T(8,128)S(1)} %reduce_sum.529), channel_id=1, replica_groups=mesh['outer'=2,'sec'=8,'tp'=2] {'tp'}, use_global_device_ids=true, to_apply=%region_13.14 | all-reduce | flops 576 | bytes 4608 | tf_op jit(solution)/shard_map/psum | solution.py:75
  570.7 9.6 %multiply_reduce_fusion.1 = (f32[1536]{0:T(1024)S(1)}, f32[1536]{0:T(1024)S(1)}, f32[1536]{0:T(1024)S(1)}, f32[1536]{0:T(1024)S(1)}, f32[1536]{0:T(1024)S(1)}, /...) fusion(f32[2,12,12,1536]{3,2,1,0:T(8,128)S(1)} %convert_multipl, ...), kind=kLoop, calls=%fused_computation.63 | loop fusion | flops 19436544 | bytes 7200384 | tf_op jit(solution)/shard_map/reduce_sum | solution.py:85
  580.3 0.0 copy-start.1
  580.3 6.3 multiply_reduce_fusion.19
  586.6 5.4 multiply_reduce_fusion.38
  592.8 4.8 stack.207
  597.6 0.0 all-reduce.7.cloned.1.call-update
  597.6 0.0 all-reduce.9.cloned.1.call-start
  597.7 54.4 %all-reduce.7.cloned.1.call-done = f32[51,1536]{1,0:T(8,128)} async-done(((f32[51,1536]{1,0:T(8,128)}), f32[51,1536]{1,0:T(8,128)}) %all-reduce.7.cloned.1.call-update) | async-done | bytes 313360 | tf_op jit(solution)/shard_map/psum | solution.py:91
  652.0 1.7 multiply_reduce_fusion.54
  653.7 5.5 psum.70
  660.0 1.7 broadcast_multiply_fusion.1
  661.7 0.0 all-reduce.9.cloned.1.call-update
  661.7 5.5 fusion.2
  667.2 20.6 %all-reduce.9.cloned.1.call-done = f32[51,1536]{1,0:T(8,128)} async-done(((f32[51,1536]{1,0:T(8,128)}), f32[51,1536]{1,0:T(8,128)}) %all-reduce.9.cloned.1.call-update) | async-done | bytes 313360 | tf_op jit(solution)/shard_map/psum | solution.py:94
  687.9 1.0 broadcast_multiply_fusion
  688.9 0.6 slice_reduce_fusion
  689.5 0.8 reshape.170
  (73 shorter events, 0.4 us)
Async XLA Ops:
  7.2 201.4 %all-gather.3.cloned.1.call-start = ((), (), s32[]{:S(2)}) async-start(), calls=%async_computation.3 | async-start | bytes 24772608 | tf_op jit(solution)/shard_map/all_gather | solution.py:53
  11.6 0.7 copy-start.9
  11.6 1.0 copy-start.2
  11.6 2.6 copy-start
  11.7 306.2 %reduce-scatter.2.cloned.1.call-start = ((), (), s32[]{:S(2)}) async-start(), calls=%async_computation.4 | async-start | bytes 12386304 | tf_op jit(solution)/shard_map/reduce_scatter | solution.py:55
  47.9 0.6 copy-start.3
  47.9 0.6 copy-start.5
  325.5 5.0 copy-start.10
  325.5 58.1 %all-to-all-start = ((bf16[8,36,3584]{2,1,0:T(8,128)(2,1)}), bf16[8,36,3584]{2,1,0:T(8,128)(2,1)}, u32[]{:S(2)}, u32[]{:S(2)}) async-start(bf16[8,36,3584]{2,1,0:T(8,128)(2,1)} %all_to_all.14), calls=%async_computation.1 | async-start | bytes 4587520 | tf_op jit(solution)/shard_map/all_to_all | solution.py:58
  330.3 213.5 %all-gather.5.cloned.1.call-start = ((), (), s32[]{:S(2)}) async-start(), calls=%async_computation.5 | async-start | bytes 6193152 | tf_op jit(solution)/shard_map/all_gather | solution.py:71
  387.7 9.2 %copy-start.7 = (f32[3584]{0:T(1024)S(1)}, f32[3584]{0:T(1024)}, u32[]{:S(2)}) copy-start(f32[3584]{0:T(1024)} %param.18) | copy-start | bytes 43012
  485.6 58.1 %copy-start.8 = (f32[1536]{0:T(1024)S(1)}, f32[1536]{0:T(1024)}, u32[]{:S(2)}) copy-start(f32[1536]{0:T(1024)} %param.13) | copy-start | bytes 18436
  489.6 162.4 %all-reduce.7.cloned.1.call-start = ((), (), s32[]{:S(2)}) async-start(), calls=%async_computation.6 | async-start | bytes 688128 | tf_op jit(solution)/shard_map/psum | solution.py:91
  557.0 2.8 copy-start.4
  557.0 2.8 copy-start.6
  580.3 6.4 copy-start.1
  597.6 90.2 %all-reduce.9.cloned.1.call-start = ((), (), s32[]{:S(2)}) async-start(), calls=%async_computation.7 | async-start | bytes 688128 | tf_op jit(solution)/shard_map/psum | solution.py:94
Sparse Core Ops, SparseCore 0:
  11.8 196.7 all-gather.2
  221.8 96.0 reduce-scatter.1
  489.8 53.9 all-gather.4
  597.7 54.2 all-reduce.6
  661.8 25.9 all-reduce.8
where the time goes:
time: 698 us; the launch traced here: 697 us
  waiting for transfers between devices  434 us (62%)
  blocking collectives  85.4 us (12%)
  other arithmetic  78 us (11%)
  local copies, waits for them, and re-layouts  53.2 us (8%)
  matrix products  26.4 us (4%)
  between operations  15 us (2%)
    all_gather x1, waiting for transfers between devices, on_device(): whole_weight = lax.all_gather(projector, 'sec', axis=1, tiled=True)  155 us
    reduce_scatter x1, waiting for transfers between devices, on_device(): lax.psum_scatter(partial_value, 'tp', scatter_dimension=1, tiled=True)  96.2 us
    all_to_all x1, blocking collectives, on_device(): lax.all_to_all(picked, 'sec', split_axis=0, concat_axis=0, tiled=True)  57.6 us
    psum x1, waiting for transfers between devices, on_device(): pod_sum = lax.psum(local_delta, 'sec')  54.4 us
    all_gather x1, waiting for transfers between devices, on_device(): full_grad = lax.all_gather(returned, 'tp', axis=1, tiled=True)  54 us
    all_to_all x1, waiting for transfers between devices, on_device(): lax.all_to_all(visual, 'sec', split_axis=0, concat_axis=0, tiled=True)  53.1 us
    reduce_sum x1, other arithmetic, on_device(): jnp.sum(conv_out, axis=-1)  23.6 us
    reduce_sum x3, other arithmetic, on_device(): kernel_rows.append(jnp.sum(window * grad_conv, axis=(0, 1, 2)))  21.3 us
  transfers between devices with their start and end apart: 6, of which 6 were waited for; matrix products, arithmetic and copies ran while one was open for 5% of the time, Pallas kernels for 0%

commit v1 on v0

--- a/solution.py
+++ b/solution.py
@@ -88,7 +88,10 @@
     local_delta = jnp.stack(kernel_rows + [gain_grad, bias_grad], axis=0)
     pods = lax.axis_size("outer")
     entries = 51 * channels
-    pod_sum = lax.psum(local_delta, "sec")
+    size, pod_sum = (lax.axis_size("sec"), local_delta)
+    for far in [1 << k for k in range(size.bit_length() - 1)]:
+        pairs = [(i, i ^ far) for i in range(size)]
+        pod_sum = pod_sum + lax.ppermute(pod_sum, "sec", pairs)
     norm_sq = lax.psum(jnp.sum(pod_sum * pod_sum), "tp")
     factor = jnp.minimum(1.0, 1.0 / jnp.sqrt(norm_sq / entries + 1e-06))
     average = lax.psum(pod_sum * factor, "outer") / pods

time: 698 us -> 667 us (0.956)
  waiting for transfers between devices: 434 us -> 404 us
    psum x1 -> x0, waiting for transfers between devices: 54.4 us -> none  [on_device(): pod_sum = lax.psum(local_delta, 'sec')]
    ppermute x0 -> x3, waiting for transfers between devices: none -> 24.9 us  [on_device(): pod_sum = pod_sum + lax.ppermute(pod_sum, 'sec', pairs)]
  transfers between devices with their start and end apart: 6 -> 8, of which waited for: 6 -> 8; matrix products, arithmetic and copies ran while one was open for 5% -> 5% of each run, Pallas kernels for 0% -> 0%
where the time goes in v1:
time: 667 us; the launch traced here: 666 us
  waiting for transfers between devices  404 us (61%)
  blocking collectives  85.4 us (13%)
  other arithmetic  76.1 us (11%)
  local copies, waits for them, and re-layouts  48.9 us (7%)
  matrix products  26.4 us (4%)
  between operations  15.1 us (2%)
  starting transfers between devices  9.65 us (1%)
    all_gather x1, waiting for transfers between devices, on_device(): whole_weight = lax.all_gather(projector, 'sec', axis=1, tiled=True)  155 us
    reduce_scatter x1, waiting for transfers between devices, on_device(): lax.psum_scatter(partial_value, 'tp', scatter_dimension=1, tiled=True)  96.2 us
    all_to_all x1, blocking collectives, on_device(): lax.all_to_all(picked, 'sec', split_axis=0, concat_axis=0, tiled=True)  57.6 us
    all_gather x1, waiting for transfers between devices, on_device(): full_grad = lax.all_gather(returned, 'tp', axis=1, tiled=True)  54 us
    all_to_all x1, waiting for transfers between devices, on_device(): lax.all_to_all(visual, 'sec', split_axis=0, concat_axis=0, tiled=True)  53.1 us
    ppermute x3, waiting for transfers between devices, on_device(): pod_sum = pod_sum + lax.ppermute(pod_sum, 'sec', pairs)  24.9 us
    reduce_sum x1, other arithmetic, on_device(): jnp.sum(conv_out, axis=-1)  23.6 us
    reduce_sum x3, other arithmetic, on_device(): kernel_rows.append(jnp.sum(window * grad_conv, axis=(0, 1, 2)))  21.3 us
  transfers between devices with their start and end apart: 8, of which 8 were waited for; matrix products, arithmetic and copies ran while one was open for 5% of the time, Pallas kernels for 0%

profile of v1, /device:TPU:0, one launch (start us, length us, event | category | flops | bytes accessed | tf_op | source)
XLA Modules:
  0.0 665.5 jit_solution(16785646092002685367)
XLA Ops:
  7.2 0.0 all-gather.3.cloned.1.call-start
  7.2 4.4 copy.22
  11.6 0.0 all-gather.3.cloned.1.call-update
  11.7 0.0 reduce-scatter.2.cloned.1.call-start
  11.7 0.6 copy-done.9
  12.3 0.2 slice_reduce_fusion.52
  12.5 0.1 copy-done.2
  12.6 0.2 slice_reduce_fusion.48
  12.8 0.3 slice_reduce_fusion.50
  13.1 0.9 slice_reduce_fusion.49
  14.0 0.1 iota_compare_fusion
  14.1 0.1 and_convert_fusion
  14.2 0.2 convert_multiply_fusion.5
  14.4 23.6 %fusion.8 = (f32[2,12,12]{2,1,0:T(8,128)S(1)}, f32[2,12,12]{2,1,0:T(8,128)S(1)}, f32[2,12,12,1536]{3,2,1,0:T(8,128)}) fusion(f32[1536]{0:T(1024)S(1)} %get-tuple-element.110, f32[1536]{0:T(1024)S(1)} %get-tuple-element.111, f32[1536]{0:T(1024)S(1)} %get-tuple-element.64, f32[1536]{0:T(1024)S(1)} %get-tuple-element.65, f32[1536]{0:T(1024)S(1)} %get-tuple-element.66, ...), kind=kLoop, calls=%fused_computation.189 | loop fusion | flops 44236224 | bytes 3842304 | tf_op jit(solution)/shard_map/reduce_sum | solution.py:43
  38.1 9.8 %all-reduce.3 = (f32[2,12,12]{2,1,0:T(8,128)S(1)}, f32[2,12,12]{2,1,0:T(8,128)S(1)}) all-reduce(f32[2,12,12]{2,1,0:T(8,128)S(1)} %get-tuple-element.58, f32[2,12,12]{2,1,0:T(8,128)S(1)} %get-tuple-element.57), channel_id=1, replica_groups=mesh['outer'=2,'sec'=8,'tp'=2] {'tp'}, use_global_device_ids=true, to_apply=%region_3.4 | all-reduce | flops 576 | bytes 4608 | tf_op jit(solution)/shard_map/psum | solution.py:42
  47.9 0.6 copy-done.3
  48.5 0.0 copy-done.5
  48.5 3.5 multiply_convert_fusion
  52.0 1.1 reshape.168
  53.1 155.4 %all-gather.3.cloned.1.call-done = bf16[1536,7168]{1,0:T(8,128)(2,1)} async-done(((bf16[1536,896]{1,0:T(8,128)(2,1)}), bf16[1536,7168]{1,0:T(8,128)(2,1)}) %all-gather.3.cloned.1.call-update) | async-done | bytes 22020112 | tf_op jit(solution)/shard_map/all_gather | solution.py:53
  208.5 13.1 %fusion.9 = f32[288,7168]{1,0:T(8,128)} fusion(bf16[288,1536]{1,0:T(8,128)(2,1)} %reshape.168, bf16[1536,7168]{1,0:T(8,128)(2,1)} %all-gather.3.cloned.1.call-done), kind=kOutput, calls=%fused_computation.190 | convolution fusion | flops 6341787648 | bytes 31162368 | tf_op jit(solution)/shard_map/dot_general | solution.py:54
  221.7 0.0 reduce-scatter.2.cloned.1.call-update
  221.7 96.2 %reduce-scatter.2.cloned.1.call-done = f32[288,3584]{1,0:T(8,128)} async-done(((f32[288,7168]{1,0:T(8,128)}), f32[288,3584]{1,0:T(8,128)}) %reduce-scatter.2.cloned.1.call-update) | async-done | bytes 4128784 | tf_op jit(solution)/shard_map/reduce_scatter | solution.py:55
  317.8 3.7 convert_element_type.43
  321.6 4.0 all_to_all.14
  325.5 4.7 all-to-all-start
  330.3 0.2 all-gather.5.cloned.1.call-start
  330.5 53.1 %all-to-all-done = bf16[8,36,3584]{2,1,0:T(8,128)(2,1)} async-done(((bf16[8,36,3584]{2,1,0:T(8,128)(2,1)}), bf16[8,36,3584]{2,1,0:T(8,128)(2,1)}, u32[]{:S(2)}, u32[]{:S(2)}) %all-to-all-start) | async-done | bytes 2064416 | tf_op jit(solution)/shard_map/all_to_all | solution.py:58
  383.7 4.0 reshape.184
  387.7 9.2 %scatter_fusion = bf16[576,3584]{1,0:T(8,128)(2,1)} fusion(bf16[576,3584]{1,0:T(8,128)(2,1)} %copy.22, s32[288]{0:T(512)S(1)} %fusion.7, bf16[288,3584]{1,0:T(8,128)(2,1)} %reshape.184), kind=kCustom, calls=%fused_computation.1 | custom fusion | bytes 6194304 | tf_op jit(solution)/shard_map/scatter | solution.py:60
  396.9 5.4 fusion.6
  402.3 5.0 all-reduce.2
  407.3 6.7 %fusion.5 = bf16[576,3584]{1,0:T(8,128)(2,1)} fusion(bf16[576,3584]{1,0:T(8,128)(2,1)} %scatter_fusion, bf16[576,3584]{1,0:T(8,128)(2,1)} %param.19, f32[576]{0:T(1024)S(1)} %get-tuple-element.117, f32[576]{0:T(1024)S(1)} %get-tuple-element.126, f32[3584]{0:T(1024)S(1)} %copy-done.7, f32[576]{0:T(1024)S(1)} %get-tuple-element.127), kind=kLoop, calls=%fused_computation.59 | loop fusion | flops 18579456 | bytes 12407552 | tf_op jit(solution)/shard_map/sub | solution.py:68
  414.0 10.0 %gather_fusion = bf16[288,3584]{1,0:T(8,128)(2,1)} fusion(bf16[576,3584]{1,0:T(8,128)(2,1)} %fusion.5, s32[1024]{0:T(1024)S(1)} %pad_clamp_fusion), kind=kCustom, calls=%fused_computation | custom fusion | bytes 4129920 | tf_op jit(solution)/shard_map/gather | solution.py:69
  424.1 4.0 convert_element_type.48
  428.0 57.6 %all_to_all.21 = bf16[8,36,3584]{2,1,0:T(8,128)(2,1)} all-to-all(bf16[8,36,3584]{2,1,0:T(8,128)(2,1)} %convert_element_type.48), channel_id=1, replica_groups=mesh['outer'=2,'sec'=8,'tp'=2] {'sec'}, dimensions={0} | all-to-all | bytes 4128768 | tf_op jit(solution)/shard_map/all_to_all | solution.py:70
  485.6 4.0 all_to_all.18
  489.6 0.0 all-gather.5.cloned.1.call-update
  489.6 0.0 all-reduce.6.cloned.1.call-start
  489.7 0.1 reshape.171
  489.8 54.0 %all-gather.5.cloned.1.call-done = bf16[288,7168]{1,0:T(8,128)(2,1)} async-done(((bf16[288,3584]{1,0:T(8,128)(2,1)}), bf16[288,7168]{1,0:T(8,128)(2,1)}) %all-gather.5.cloned.1.call-update) | async-done | bytes 4128784 | tf_op jit(solution)/shard_map/all_gather | solution.py:71
  543.7 13.2 %multiply_reduce_fusion.53 = (f32[1536]{0:T(1024)S(1)}, f32[288]{0:T(512)S(1)}, f32[288,1536]{1,0:T(8,128)}) fusion(f32[288]{0:T(512)S(1)} %reshape.171, f32[1536]{0:T(1024)S(1)} %copy-done.8, bf16[288,7168]{1,0:T(8,128)(2,1)} %all-gather.5.cloned.1.call-done, bf16[1536,7168]{1,0:T(8,128)(2,1)} %all-gather.3.cloned.1.call-done), kind=kOutput, calls=%fused_computation.120 | convolution fusion | flops 6343555072 | bytes 27932928 | tf_op jit(solution)/shard_map/dot_general | solution.py:72
  557.0 2.8 reshape.169
  559.8 3.4 multiply_reduce_fusion
  563.1 0.1 reduce_sum.529
  563.2 7.4 %all-reduce.1 = (f32[2,12,12]{2,1,0:T(8,128)S(1)}, f32[2,12,12]{2,1,0:T(8,128)S(1)}) all-reduce(f32[2,12,12]{2,1,0:T(8,128)S(1)} %get-tuple-element.5, f32[2,12,12]{2,1,0:T(8,128)S(1)} %reduce_sum.529), channel_id=1, replica_groups=mesh['outer'=2,'sec'=8,'tp'=2] {'tp'}, use_global_device_ids=true, to_apply=%region_13.14 | all-reduce | flops 576 | bytes 4608 | tf_op jit(solution)/shard_map/psum | solution.py:75
  570.7 9.6 %multiply_reduce_fusion.1 = (f32[1536]{0:T(1024)S(1)}, f32[1536]{0:T(1024)S(1)}, f32[1536]{0:T(1024)S(1)}, f32[1536]{0:T(1024)S(1)}, f32[1536]{0:T(1024)S(1)}, /...) fusion(f32[2,12,12,1536]{3,2,1,0:T(8,128)S(1)} %convert_multipl, ...), kind=kLoop, calls=%fused_computation.63 | loop fusion | flops 19436544 | bytes 7200384 | tf_op jit(solution)/shard_map/reduce_sum | solution.py:85
  580.3 6.3 multiply_reduce_fusion.19
  586.6 5.4 multiply_reduce_fusion.38
  592.8 0.5 stack.207
  593.3 0.1 collective-permute-start
  593.4 1.6 collective-permute-done
  595.1 1.8 collective-permute-start.1
  596.9 8.4 %collective-permute-done.1 = f32[51,1536]{1,0:T(8,128)S(1)} collective-permute-done((f32[51,1536]{1,0:T(8,128)S(1)}, f32[51,1536]{1,0:T(8,128)S(1)}, u32[]{:S(2)}, u32[]{:S(2)}) %collective-permute-start.1) | collective-permute-done | bytes 313376 | tf_op jit(solution)/shard_map/ppermute | solution.py:94
  605.3 2.7 collective-permute-start.2
  608.0 14.9 %collective-permute-done.2 = f32[51,1536]{1,0:T(8,128)S(1)} collective-permute-done((f32[51,1536]{1,0:T(8,128)S(1)}, f32[51,1536]{1,0:T(8,128)S(1)}, u32[]{:S(2)}, u32[]{:S(2)}) %collective-permute-start.2) | collective-permute-done | bytes 313376 | tf_op jit(solution)/shard_map/ppermute | solution.py:94
  622.9 0.7 multiply_reduce_fusion.54
  623.6 5.5 psum.62
  629.9 0.8 broadcast_multiply_fusion.1
  630.7 5.5 fusion.2
  636.2 20.4 %all-reduce.6.cloned.1.call-done = f32[51,1536]{1,0:T(8,128)} async-done(((f32[51,1536]{1,0:T(8,128)}), f32[51,1536]{1,0:T(8,128)}) %all-reduce.6.cloned.1.call-update) | async-done | bytes 313360 | tf_op jit(solution)/shard_map/psum | solution.py:97
  656.6 1.0 broadcast_multiply_fusion
  657.6 0.6 slice_reduce_fusion
  658.2 0.8 reshape.170
  (78 shorter events, 0.5 us)
Async XLA Ops:
  7.2 201.4 %all-gather.3.cloned.1.call-start = ((), (), s32[]{:S(2)}) async-start(), calls=%async_computation.3 | async-start | bytes 24772608 | tf_op jit(solution)/shard_map/all_gather | solution.py:53
  11.6 0.7 copy-start.9
  11.6 1.0 copy-start.2
  11.6 2.6 copy-start
  11.7 306.2 %reduce-scatter.2.cloned.1.call-start = ((), (), s32[]{:S(2)}) async-start(), calls=%async_computation.4 | async-start | bytes 12386304 | tf_op jit(solution)/shard_map/reduce_scatter | solution.py:55
  47.9 0.6 copy-start.3
  47.9 0.6 copy-start.5
  325.5 5.0 copy-start.10
  325.5 58.1 %all-to-all-start = ((bf16[8,36,3584]{2,1,0:T(8,128)(2,1)}), bf16[8,36,3584]{2,1,0:T(8,128)(2,1)}, u32[]{:S(2)}, u32[]{:S(2)}) async-start(bf16[8,36,3584]{2,1,0:T(8,128)(2,1)} %all_to_all.14), calls=%async_computation.1 | async-start | bytes 4587520 | tf_op jit(solution)/shard_map/all_to_all | solution.py:58
  330.3 213.5 %all-gather.5.cloned.1.call-start = ((), (), s32[]{:S(2)}) async-start(), calls=%async_computation.5 | async-start | bytes 6193152 | tf_op jit(solution)/shard_map/all_gather | solution.py:71
  387.6 9.2 %copy-start.7 = (f32[3584]{0:T(1024)S(1)}, f32[3584]{0:T(1024)}, u32[]{:S(2)}) copy-start(f32[3584]{0:T(1024)} %param.18) | copy-start | bytes 43012
  485.6 58.1 %copy-start.8 = (f32[1536]{0:T(1024)S(1)}, f32[1536]{0:T(1024)}, u32[]{:S(2)}) copy-start(f32[1536]{0:T(1024)} %param.13) | copy-start | bytes 18436
  489.6 167.0 %all-reduce.6.cloned.1.call-start = ((), (), s32[]{:S(2)}) async-start(), calls=%async_computation.6 | async-start | bytes 688128 | tf_op jit(solution)/shard_map/psum | solution.py:97
  557.0 2.8 copy-start.4
  557.0 2.8 copy-start.6
  580.3 6.4 copy-start.1
  593.3 1.7 collective-permute-start
  595.1 10.2 %collective-permute-start.1 = (f32[51,1536]{1,0:T(8,128)S(1)}, f32[51,1536]{1,0:T(8,128)S(1)}, u32[]{:S(2)}, u32[]{:S(2)}) collective-permute-start(f32[51,1536]{1,0:T(8,128)S(1)} %add.263), channel_id=1, source_target_pairs={{0,4},{2,6},{4,0},{6,2},{8,12},{10,14},{12,8},{14,10},{1,5},{3,7},... | collective-permute-start | bytes 940040 | tf_op jit(solution)/shard_map/ppermute | solution.py:94
  605.3 17.6 %collective-permute-start.2 = (f32[51,1536]{1,0:T(8,128)S(1)}, f32[51,1536]{1,0:T(8,128)S(1)}, u32[]{:S(2)}, u32[]{:S(2)}) collective-permute-start(f32[51,1536]{1,0:T(8,128)S(1)} %add.264), channel_id=1, source_target_pairs={{0,8},{2,10},{4,12},{6,14},{8,0},{10,2},{12,4},{14,6},{1,9},{3,11}... | collective-permute-start | bytes 940040 | tf_op jit(solution)/shard_map/ppermute | solution.py:94
Sparse Core Ops, SparseCore 0:
  11.8 196.7 all-gather.2
  221.8 96.0 reduce-scatter.1
  489.8 53.9 all-gather.4
  630.8 25.7 all-reduce.5
